TPU v7x, 32 devices: a whole 2x2x4 slice. The times are simulated.
32 devices in a mesh: shots: 2 (over x), gx: 16 (over z, y, core).
Axes of the slice: x: 2, y: 2, z: 4, core: 2. Of those that a mesh axis runs over, the one named last changes fastest.
Arguments:
- courant_sq: float32 [128, 128, 128], P('gx'), may hold values from 0.03 to 0.2
- wave_prev: float32 [256, 128, 128], P(('shots', 'gx')), parts along dimension 0, may hold values from -6 to 6
- wave_now: float32 [256, 128, 128], P(('shots', 'gx')), parts along dimension 0, may hold values from -6 to 6
- adj_late: float32 [256, 128, 128], P(('shots', 'gx')), parts along dimension 0, may hold values from -6 to 6
- adj_last: float32 [256, 128, 128], P(('shots', 'gx')), parts along dimension 0, may hold values from -6 to 6
- wavelet: float32 [24], P('shots'), parts along dimension 0, may hold values from -48 to 48
- source_cell: int32 [2], P('shots'), parts along dimension 0, may hold values from 0 to 2097151
- receivers: int32 [2048], P('shots'), parts along dimension 0, may hold values from 0 to 2097151
- observed: float32 [24, 1024], P('shots'), parts along dimension 0, may hold values from -6 to 6
- footprint: int32 [4096], P(('shots', 'gx')), parts along dimension 0, may hold values 0 or 1
- brick_owner: int32 [2048, 1], P('gx'), may hold values from 0 to 15; in each aligned block of 128 rows (0 to 127, 128 to 255, ...) at most 16 rows name the same one
- prior_in: bfloat16 [32, 27], replicated, may hold values from -1.25 to 1.25
- prior_in_bias: float32 [32], replicated, may hold values from -3 to 3
- prior_mix: bfloat16 [32, 32], replicated, may hold values from -1 to 1
- prior_mix_bias: float32 [32], replicated, may hold values from -3 to 3
- prior_out: bfloat16 [27, 32], replicated, may hold values from -0.21875 to 0.21875
- prior_out_bias: float32 [1], replicated, may hold values from -3 to 3
Outputs:
- residual_traces: float32 [24, 1024], P('shots'), parts along dimension 0
- owned_bricks: bfloat16 [32, 16, 16, 1024], P(('shots', 'gx')), parts along dimension 0
There are 2 independent parts, one for each index of `shots`. A program takes and returns all parts, laid end to end along the dimension named above; an argument that names none is the same for every part. Nothing has to cross between parts.
Inputs may be any that keep to these rules, and one draw needn't show every extreme that they name: `brick_owner`: among the 128 bricks of one device's block, at most 16 have the same owner.
All inputs are finite; a program needn't handle non-finite values. No bound on the sum of `footprint` on one device may be relied on, other than what follows from the above.
Results may differ from a plain program's by a relative error of at most 0.0045.
Values may be sent and summed in bfloat16 or wider, within the bound.
A program may use at most 128 MiB of HBM per device.

v0:
```python
import functools
import jax
import jax.numpy as jnp
import numpy as np
from jax import lax
from jax.experimental import pallas as pl
from jax.experimental.pallas import tpu as pltpu
from jax.sharding import PartitionSpec as P

MESH = pl.DeviceIdType.MESH
PAD = 8


def wave_kernel(
    n,
    c_ref,
    wave_prev,
    wave_now,
    adj_late,
    adj_last,
    wavelet,
    source,
    row_lane,
    z_lane,
    row_sub,
    z_sub,
    observed,
    grad_ref,
    wide_ref,
    resid_ref,
    fwd,
    adj,
    changes,
    c12,
    src,
    inj,
    hot,
    hot_t,
    zhot,
    zhot_t,
    parts,
    inj_parts,
    rec_send,
    rec_recv,
    resid8,
    f_send,
    f_recv,
    a_send,
    a_recv,
    r_send,
    r_recv,
    g_send,
    g_recv,
):
    cx, ny, nz = c_ref.shape
    steps = changes.shape[0]
    nrec = row_lane.shape[1]
    groups = nrec // 128
    rows = cx * ny
    me = lax.axis_index("gx")
    shot = lax.axis_index("shots")

    barrier = pltpu.get_barrier_semaphore()

    for buf in (fwd, adj):
        for k in range(3):
            buf[k] = jnp.zeros(buf.shape[1:], jnp.float32)
    wide_ref[0:2] = jnp.zeros((2, ny, nz), jnp.bfloat16)
    wide_ref[cx + 2 : cx + 4] = jnp.zeros((2, ny, nz), jnp.bfloat16)
    def greet(d, carry):
        pl.semaphore_signal(
            barrier, inc=1, device_id=(shot, lax.rem(me + d, n)), device_id_type=MESH
        )
        return carry

    lax.fori_loop(1, n, greet, 0)

    inner = pl.ds(PAD, ny)
    for i in range(cx):
        fwd[0, i + 2, inner] = wave_prev[i]
        fwd[1, i + 2, inner] = wave_now[i]
        adj[0, i + 2, inner] = adj_late[i]
        adj[1, i + 2, inner] = adj_last[i]
    pl.semaphore_wait(barrier, n - 1)

    def halo(buf, k, send, recv, up):
        lo = cx if up else 2
        to = 0 if up else cx + 2
        side = 1 if up else 0
        return pltpu.make_async_remote_copy(
            src_ref=buf.at[k, pl.ds(lo, 2), inner],
            dst_ref=buf.at[k, pl.ds(to, 2), inner],
            send_sem=send.at[side],
            recv_sem=recv.at[k, side],
            device_id=(shot, me + 1 if up else me - 1),
            device_id_type=MESH,
        )

    def start_side(buf, k, send, recv, up):
        @pl.when((me < n - 1) if up else (me > 0))
        def _():
            halo(buf, k, send, recv, up).start()

    def wait_side(buf, k, send, recv):
        @pl.when(me < n - 1)
        def _():
            halo(buf, k, send, recv, True).wait_send()
            halo(buf, k, send, recv, False).wait_recv()

        @pl.when(me > 0)
        def _():
            halo(buf, k, send, recv, False).wait_send()
            halo(buf, k, send, recv, True).wait_recv()

    for up in (False, True):
        start_side(fwd, 1, f_send, f_recv, up)
    for up in (False, True):
        start_side(adj, 1, a_send, a_recv, up)

    for i in range(cx):
        c12[i] = c_ref[i] * (1.0 / 12.0)
    y_at = lax.broadcasted_iota(jnp.int32, (ny, nz), 0)
    z_at = lax.broadcasted_iota(jnp.int32, (ny, nz), 1)
    for i in range(cx):
        flat = ((me * cx + i) * ny + y_at) * nz + z_at
        src[i] = jnp.where(flat == source[0], 1.0, 0.0)

    def build(j, carry):
        at = pl.ds(pl.multiple_of(j * 128, 128), 128)
        r_iota = lax.broadcasted_iota(jnp.int32, (128, nrec), 0) + j * 128
        hot[at, :] = jnp.where(r_iota == row_lane[...], 1.0, 0.0).astype(jnp.bfloat16)
        return carry

    lax.fori_loop(0, rows // 128, build, 0)

    def build_t(j, carry):
        at = pl.ds(pl.multiple_of(j * 128, 128), 128)
        r_iota = lax.broadcasted_iota(jnp.int32, (128, rows), 1)
        hot_t[at, :] = jnp.where(r_iota == row_sub[at, :], 1.0, 0.0).astype(jnp.bfloat16)
        lane = lax.broadcasted_iota(jnp.int32, (128, nz), 1)
        zhot[at, :] = jnp.where(lane == z_sub[at, :], 1.0, 0.0)
        return carry

    lax.fori_loop(0, groups, build_t, 0)
    zhot_t[...] = jnp.where(
        lax.broadcasted_iota(jnp.int32, (nz, nrec), 0) == z_lane[...], 1.0, 0.0
    )

    chunk = 32
    lane = lax.broadcasted_iota(jnp.int32, (chunk, nz), 1)

    def laplace12(buf, k, i, y):
        def at(plane, dy):
            return buf[k, plane, pl.ds(PAD + y + dy, chunk), :]

        mid = at(i + 2, 0)
        near = (at(i + 3, 0) + at(i + 1, 0)) + (at(i + 2, 1) + at(i + 2, -1))
        far = (at(i + 4, 0) + at(i, 0)) + (at(i + 2, 2) + at(i + 2, -2))
        near += jnp.where(lane >= 1, pltpu.roll(mid, 1, 1), 0.0)
        near += jnp.where(lane < nz - 1, pltpu.roll(mid, nz - 1, 1), 0.0)
        far += jnp.where(lane >= 2, pltpu.roll(mid, 2, 1), 0.0)
        far += jnp.where(lane < nz - 2, pltpu.roll(mid, nz - 2, 1), 0.0)
        return mid, 16.0 * near - far - 90.0 * mid

    order = [0, 1, cx - 2, cx - 1] + list(range(2, cx - 2))

    def send_records(t):
        def one(d, carry):
            pltpu.make_async_remote_copy(
                src_ref=rec_send.at[t],
                dst_ref=rec_recv.at[t, d - 1],
                send_sem=r_send.at[t],
                recv_sem=r_recv.at[t],
                device_id=(shot, lax.rem(me + d, n)),
                device_id_type=MESH,
            ).start()
            return carry

        lax.fori_loop(1, n, one, 0)

    def forward(t, carry):
        prev, cur, nxt = lax.rem(t, 3), lax.rem(t + 1, 3), lax.rem(t + 2, 3)
        impulse = wavelet[t]
        wait_side(fwd, cur, f_send, f_recv)
        for done, i in enumerate(order):
            for y in range(0, ny, chunk):
                mid, lap = laplace12(fwd, cur, i, y)
                at = pl.ds(y, chunk)
                change = c12[i, at] * lap + impulse * src[i, at]
                changes[t, i, at] = change
                newest = 2.0 * mid - fwd[prev, i + 2, pl.ds(PAD + y, chunk)] + change
                fwd[nxt, i + 2, pl.ds(PAD + y, chunk)] = newest
                high = newest.astype(jnp.bfloat16)
                parts[pl.ds(i * ny + y, chunk), 0:nz] = high
                parts[pl.ds(i * ny + y, chunk), nz : 2 * nz] = (
                    newest - high.astype(jnp.float32)
                ).astype(jnp.bfloat16)
            if done == 1:

                @pl.when(t < steps - 1)
                def _():
                    start_side(fwd, nxt, f_send, f_recv, False)

            if done == 3:

                @pl.when(t < steps - 1)
                def _():
                    start_side(fwd, nxt, f_send, f_recv, True)

        picked = jnp.dot(hot_t[...], parts[...], preferred_element_type=jnp.float32)
        zsel = zhot[...]
        ones = jnp.ones((8, nz), jnp.bfloat16)
        total = jnp.zeros((8, nrec), jnp.float32)
        for h in range(2):
            kept = (picked[:, h * nz : (h + 1) * nz] * zsel).astype(jnp.bfloat16)
            total += lax.dot_general(
                ones, kept, (((1,), (1,)), ((), ())), preferred_element_type=jnp.float32
            )
        for g in range(groups):
            rec_send[t, g : g + 1, :] = total[0:1, g * 128 : (g + 1) * 128]
        send_records(t)
        return carry

    lax.fori_loop(0, steps, forward, 0)

    for i in range(cx):
        grad_ref[i] = jnp.zeros((ny, nz), jnp.float32)

    def backward(s, carry):
        t = steps - 1 - s
        prev, cur, nxt = lax.rem(s, 3), lax.rem(s + 1, 3), lax.rem(s + 2, 3)
        arrived = rec_recv.at[t]
        pltpu.make_async_copy(arrived, arrived, r_recv.at[t]).wait()
        pltpu.make_async_copy(arrived, arrived, r_send.at[t]).wait()
        total = rec_send[t] + jnp.sum(rec_recv[t], axis=0)
        misfit = total - observed[t]
        resid_ref[t] = misfit
        resid8[...] = misfit
        for g in range(groups):
            at = pl.ds(g * 128, 128)
            value = zhot_t[:, at] * resid8[g : g + 1, :]
            high = value.astype(jnp.bfloat16)
            inj_parts[pl.ds(0, nz), at] = high
            inj_parts[pl.ds(nz, nz), at] = (value - high.astype(jnp.float32)).astype(jnp.bfloat16)
        spread = lax.dot_general(
            hot[...], inj_parts[...], (((1,), (1,)), ((), ())), preferred_element_type=jnp.float32
        )
        inj[...] = spread[:, 0:nz] + spread[:, nz : 2 * nz]
        wait_side(adj, cur, a_send, a_recv)
        for done, i in enumerate(order):
            for y in range(0, ny, chunk):
                mid, lap = laplace12(adj, cur, i, y)
                at = pl.ds(y, chunk)
                newest = (
                    2.0 * mid
                    - adj[prev, i + 2, pl.ds(PAD + y, chunk)]
                    + (c12[i, at] * lap + inj[pl.ds(i * ny + y, chunk), :])
                )
                adj[nxt, i + 2, pl.ds(PAD + y, chunk)] = newest
                grad_ref[i, at] = grad_ref[i, at] + newest * changes[t, i, at]
            if done == 1:

                @pl.when(s < steps - 1)
                def _():
                    start_side(adj, nxt, a_send, a_recv, False)

            if done == 3:

                @pl.when(s < steps - 1)
                def _():
                    start_side(adj, nxt, a_send, a_recv, True)

        return carry

    lax.fori_loop(0, steps, backward, 0)

    for i in range(cx):
        wide_ref[i + 2] = grad_ref[i].astype(jnp.bfloat16)

    def edge(up):
        side = 1 if up else 0
        return pltpu.make_async_remote_copy(
            src_ref=wide_ref.at[pl.ds(cx if up else 2, 2)],
            dst_ref=wide_ref.at[pl.ds(0 if up else cx + 2, 2)],
            send_sem=g_send.at[side],
            recv_sem=g_recv.at[side],
            device_id=(shot, me + 1 if up else me - 1),
            device_id_type=MESH,
        )

    @pl.when(me < n - 1)
    def _():
        edge(True).start()

    @pl.when(me > 0)
    def _():
        edge(False).start()

    @pl.when(me < n - 1)
    def _():
        edge(True).wait_send()
        edge(False).wait_recv()

    @pl.when(me > 0)
    def _():
        edge(False).wait_send()
        edge(True).wait_recv()


def wave(n, c, wave_prev, wave_now, adj_late, adj_last, wavelet, source, receivers, observed):
    cx, ny, nz = c.shape
    steps, nrec = observed.shape
    rows = cx * ny
    relative = receivers - lax.axis_index("gx") * (rows * nz)
    inside = (relative >= 0) & (relative < rows * nz)
    row = jnp.where(inside, relative // nz, -1)
    z = jnp.where(inside, relative % nz, -1)
    vmem = pl.BlockSpec(memory_space=pltpu.VMEM)
    smem = pl.BlockSpec(memory_space=pltpu.SMEM)
    groups = nrec // 128
    f32, bf16 = jnp.float32, jnp.bfloat16
    grad, wide, resid = pl.pallas_call(
        functools.partial(wave_kernel, n),
        out_shape=(
            jax.ShapeDtypeStruct((cx, ny, nz), f32),
            jax.ShapeDtypeStruct((cx + 4, ny, nz), bf16),
            jax.ShapeDtypeStruct((steps, groups, 128), f32),
        ),
        in_specs=[vmem] * 5 + [smem] * 2 + [vmem] * 5,
        out_specs=(vmem, vmem, vmem),
        scratch_shapes=[
            pltpu.VMEM((3, cx + 4, ny + 2 * PAD, nz), f32),
            pltpu.VMEM((3, cx + 4, ny + 2 * PAD, nz), f32),
            pltpu.VMEM((steps, cx, ny, nz), f32),
            pltpu.VMEM((cx, ny, nz), f32),
            pltpu.VMEM((cx, ny, nz), f32),
            pltpu.VMEM((rows, nz), f32),
            pltpu.VMEM((rows, nrec), bf16),
            pltpu.VMEM((nrec, rows), bf16),
            pltpu.VMEM((nrec, nz), f32),
            pltpu.VMEM((nz, nrec), f32),
            pltpu.VMEM((rows, 2 * nz), bf16),
            pltpu.VMEM((2 * nz, nrec), bf16),
            pltpu.VMEM((steps, groups, 128), f32),
            pltpu.VMEM((steps, n - 1, groups, 128), f32),
            pltpu.VMEM((groups, 128), f32),
            pltpu.SemaphoreType.DMA((2,)),
            pltpu.SemaphoreType.DMA((3, 2)),
            pltpu.SemaphoreType.DMA((2,)),
            pltpu.SemaphoreType.DMA((3, 2)),
            pltpu.SemaphoreType.DMA((steps,)),
            pltpu.SemaphoreType.DMA((steps,)),
            pltpu.SemaphoreType.DMA((2,)),
            pltpu.SemaphoreType.DMA((2,)),
        ],
        compiler_params=pltpu.CompilerParams(
            collective_id=0, has_side_effects=True, vmem_limit_bytes=56 * 2**20
        ),
        name="wave",
    )(
        c,
        wave_prev,
        wave_now,
        adj_late,
        adj_last,
        wavelet,
        source,
        row[None, :],
        z[None, :],
        row[:, None],
        z[:, None],
        observed.reshape(steps, groups, 128),
    )
    return grad, wide, resid.reshape(steps, nrec)


def prior_kernel(wide, grad, w1, w2, w3, b1, b2, b3, model_ref, planes, shifted, acc, bias1, bias2):
    cx, ny, nz = grad.shape
    deep = planes.shape[0] // ny
    span = 4
    planes[...] = jnp.zeros(planes.shape, jnp.float32)
    for x in range(cx + 4):
        planes[pl.ds(x, ny, stride=deep), :] = wide[x].astype(jnp.float32)
    shifted[0] = jnp.zeros(shifted.shape[1:], jnp.bfloat16)
    shifted[ny + 1] = jnp.zeros(shifted.shape[1:], jnp.bfloat16)
    acc[...] = jnp.zeros(acc.shape, jnp.float32)
    bias1[...] = jnp.broadcast_to(b1[...], bias1.shape)
    bias2[...] = jnp.broadcast_to(b2[...], bias2.shape)
    block = 8
    lane = lax.broadcasted_iota(jnp.int32, (block * deep, nz), 1)

    def shift(j, carry):
        v = planes[pl.ds(pl.multiple_of(j * block * deep, block * deep), block * deep), :]
        ahead = jnp.where(lane >= 1, pltpu.roll(v, 1, 1), 0.0)
        behind = jnp.where(lane < nz - 1, pltpu.roll(v, nz - 1, 1), 0.0)
        for c, part in enumerate((ahead, v, behind)):
            shifted[pl.ds(1 + j * block, block), c] = part.astype(jnp.bfloat16).reshape(
                block, deep, nz
            )
        return carry

    lax.fori_loop(0, ny // block, shift, 0)
    half = w2.shape[0]
    rest = w1.shape[0] - half
    small = lax.broadcasted_iota(jnp.int32, (cx, nz), 1)

    def rows(j, carry):
        y0 = j * span
        cells = jnp.concatenate(
            [shifted[pl.ds(y0 + k, 3)].reshape(9 * deep, nz) for k in range(span)], axis=1
        )
        lifted = jnp.dot(w1[...], cells, preferred_element_type=jnp.float32) + bias1[...]
        lifted = jnp.maximum(lifted, 0.0).astype(jnp.bfloat16)
        hidden = jnp.concatenate(
            [
                jnp.dot(w2[...], lifted[:half], preferred_element_type=jnp.float32),
                jnp.dot(w2[:rest, :rest], lifted[half:], preferred_element_type=jnp.float32),
            ],
            axis=0,
        )
        hidden = jnp.maximum(hidden + bias2[...], 0.0).astype(jnp.bfloat16)
        out = jnp.dot(w3[...], hidden, preferred_element_type=jnp.float32)
        for k in range(span):
            for b in range(3):
                c0, c1, c2 = [
                    out[(3 * b + c) * cx : (3 * b + c + 1) * cx, k * nz : (k + 1) * nz]
                    for c in range(3)
                ]
                total = c1 + jnp.where(small >= 1, pltpu.roll(c0, 1, 1), 0.0)
                total += jnp.where(small < nz - 1, pltpu.roll(c2, nz - 1, 1), 0.0)
                at = pl.ds(pl.multiple_of((y0 + k + 2 - b) * cx, cx), cx)
                acc[at, :] = acc[at, :] + total
        return carry

    lax.fori_loop(0, ny // span, rows, 0)
    for x in range(cx):
        conv = acc[pl.ds(cx + x, ny, stride=cx), :] + b3[0]
        model_ref[x] = (grad[x] + conv).astype(jnp.bfloat16)


def prior(wide, grad, weight_in, bias_in, weight_mix, bias_mix, weight_out, bias_out):
    cx, ny, nz = grad.shape
    ch = weight_in.shape[0]
    bf16, f32 = jnp.bfloat16, jnp.float32
    deep = 16
    held = cx + 2
    near = np.zeros((held, 3, deep), np.float32)
    far = np.zeros((cx, 3, held), np.float32)
    for a in range(3):
        for x in range(held):
            near[x, a, x + a] = 1.0
        for x in range(cx):
            far[x, a, x + a] = 1.0
    w1 = jnp.einsum("xai,hak->xhki", near.astype(bf16), weight_in.reshape(ch, 3, 9))
    w1 = w1.reshape(held * ch, 9 * deep)
    w2 = jnp.einsum("xi,hk->xhik", np.eye(cx, dtype=np.float32).astype(bf16), weight_mix)
    w2 = w2.reshape(cx * ch, cx * ch)
    margin = lax.axis_index("gx") * cx - 1 + jnp.arange(held, dtype=jnp.int32)
    keep = (margin >= 0) & (margin < cx * lax.axis_size("gx"))
    band = jnp.where(keep[None, None], far, 0.0).astype(bf16)
    w3 = jnp.einsum("xai,akh->kxih", band, weight_out.reshape(3, 9, ch))
    w3 = w3.reshape(9 * cx, held * ch)
    b1 = jnp.tile(bias_in, held)[:, None]
    b2 = jnp.tile(bias_mix, held)[:, None]
    vmem = pl.BlockSpec(memory_space=pltpu.VMEM)
    smem = pl.BlockSpec(memory_space=pltpu.SMEM)
    return pl.pallas_call(
        prior_kernel,
        out_shape=jax.ShapeDtypeStruct((cx, ny, nz), bf16),
        in_specs=[vmem] * 7 + [smem],
        out_specs=vmem,
        scratch_shapes=[
            pltpu.VMEM((ny * deep, nz), f32),
            pltpu.VMEM((ny + 2, 3, deep, nz), bf16),
            pltpu.VMEM(((ny + 2) * cx, nz), f32),
            pltpu.VMEM((held * ch, 4 * nz), f32),
            pltpu.VMEM((held * ch, 4 * nz), f32),
        ],
        compiler_params=pltpu.CompilerParams(vmem_limit_bytes=40 * 2**20),
        name="prior",
    )(wide, grad, w1.astype(bf16), w2.astype(bf16), w3.astype(bf16), b1, b2, bias_out)


def route_kernel(n, cap, model, owner_sub, owner_lane, print_lane, out, buckets, own, send, recv):
    cx, ny, nz = model.shape
    me = lax.axis_index("gx")
    shot = lax.axis_index("shots")
    barrier = pltpu.get_barrier_semaphore()

    def greet(d, carry):
        pl.semaphore_signal(
            barrier, inc=1, device_id=(shot, lax.rem(me + d, n)), device_id_type=MESH
        )
        return carry

    lax.fori_loop(1, n, greet, 0)
    before = lax.broadcasted_iota(jnp.int32, (ny, ny), 0)
    after = lax.broadcasted_iota(jnp.int32, (ny, ny), 1)
    same = jnp.where((owner_sub[...] == owner_lane[...]) & (before < after), 1.0, 0.0)
    slots = jnp.sum(same, axis=0, keepdims=True).astype(jnp.int32)
    place = owner_lane[...] * cap + slots
    place = jnp.where(print_lane[...] == 1, place, -1)
    at = lax.broadcasted_iota(jnp.int32, (n * cap, ny), 0)
    pick = jnp.where(at == place, 1.0, 0.0).astype(jnp.bfloat16)
    for x in range(cx):
        part = jnp.dot(pick, model[x], preferred_element_type=jnp.float32).astype(jnp.bfloat16)
        buckets[:, :, x * nz : (x + 1) * nz] = part.reshape(n, cap, nz)
    pl.semaphore_wait(barrier, n - 1)

    def copy(d):
        to = lax.rem(me + d, n)
        return pltpu.make_async_remote_copy(
            src_ref=buckets.at[to],
            dst_ref=out.at[me],
            send_sem=send.at[d],
            recv_sem=recv.at[d],
            device_id=(shot, to),
            device_id_type=MESH,
        )

    def landed(d):
        source = lax.rem(me - d + n, n)
        return pltpu.make_async_copy(out.at[source], out.at[source], recv.at[d])

    mine = pltpu.make_async_copy(buckets.at[me], out.at[me], own)

    def start(d, carry):
        copy(d).start()
        return carry

    def finish(d, carry):
        copy(d).wait_send()
        landed(d).wait()
        return carry

    lax.fori_loop(1, n, start, 0)
    mine.start()
    mine.wait()
    lax.fori_loop(1, n, finish, 0)


def route(n, cap, model, owner, footprint):
    cx, ny, nz = model.shape
    vmem = pl.BlockSpec(memory_space=pltpu.VMEM)
    return pl.pallas_call(
        functools.partial(route_kernel, n, cap),
        out_shape=jax.ShapeDtypeStruct((n, cap, cx * nz), jnp.bfloat16),
        in_specs=[vmem] * 4,
        out_specs=pl.BlockSpec(memory_space=pl.ANY),
        scratch_shapes=[
            pltpu.VMEM((n, cap, cx * nz), jnp.bfloat16),
            pltpu.SemaphoreType.DMA,
            pltpu.SemaphoreType.DMA((n,)),
            pltpu.SemaphoreType.DMA((n,)),
        ],
        compiler_params=pltpu.CompilerParams(
            collective_id=1, has_side_effects=True, vmem_limit_bytes=24 * 2**20
        ),
        name="route",
    )(model, owner, owner.reshape(1, ny), footprint.reshape(1, ny))


def per_device(
    courant_sq,
    wave_prev,
    wave_now,
    adj_late,
    adj_last,
    wavelet,
    source_cell,
    receivers,
    observed,
    footprint,
    brick_owner,
    prior_in,
    prior_in_bias,
    prior_mix,
    prior_mix_bias,
    prior_out,
    prior_out_bias,
):
    cells_x, cells_y, cells_z = wave_now.shape
    devices = lax.axis_size("gx")
    grad, grad_wide, residual_traces = wave(
        devices,
        courant_sq,
        wave_prev,
        wave_now,
        adj_late,
        adj_last,
        wavelet,
        source_cell,
        receivers,
        observed,
    )
    model_grad = prior(
        grad_wide,
        grad,
        prior_in,
        prior_in_bias,
        prior_mix,
        prior_mix_bias,
        prior_out,
        prior_out_bias,
    )
    capacity = max(2, 2 * cells_y // devices)
    if capacity % 16 == 0:
        arrived = route(devices, capacity, model_grad, brick_owner, footprint)
        return (residual_traces, arrived[None])
    bricks = model_grad.transpose(1, 0, 2).reshape(cells_y, cells_x * cells_z)
    bricks = jnp.where((footprint == 1)[:, None], bricks, jnp.zeros_like(bricks))
    owners = brick_owner[:, 0]
    same = owners[:, None] == owners[None, :]
    lower = (
        jnp.arange(cells_y, dtype=jnp.int32)[:, None]
        > jnp.arange(cells_y, dtype=jnp.int32)[None, :]
    )
    slots = jnp.sum((same & lower).astype(jnp.int32), axis=1)
    buckets = (
        jnp.zeros((devices, capacity, cells_x * cells_z), jnp.bfloat16)
        .at[owners, slots]
        .set(bricks)
    )
    arrived = lax.all_to_all(buckets, "gx", split_axis=0, concat_axis=0, tiled=True)
    return (residual_traces, arrived[None])


def solution(mesh):
    return jax.shard_map(
        per_device,
        mesh=mesh,
        in_specs=(
            P("gx", None, None),
            P(("shots", "gx"), None, None),
            P(("shots", "gx"), None, None),
            P(("shots", "gx"), None, None),
            P(("shots", "gx"), None, None),
            P("shots"),
            P("shots"),
            P("shots"),
            P("shots", None),
            P(("shots", "gx")),
            P("gx", None),
            P(),
            P(),
            P(),
            P(),
            P(),
            P(),
        ),
        out_specs=(P("shots", None), P(("shots", "gx"), None, None, None)),
        check_vma=False,
    )
```

profile of v0, /device:TPU:13, one launch (start us, length us, event | category | flops | bytes accessed | tf_op | source)
XLA Modules:
  0.0 196.5 jit_solution(17975579924500723185)
XLA Ops:
  0.6 0.0 copy-start.13
  0.6 0.7 copy-done.13
  1.3 0.0 copy-start.7
  1.3 0.0 copy-start.6
  1.4 1.0 copy.27.row_sub
  2.4 0.0 copy-done.7
  2.4 0.0 copy-done.6
  2.4 0.0 copy-start.4
  2.4 1.0 copy.28.z_sub
  3.4 0.0 copy-done.4
  3.4 0.6 slice.observed
  4.7 142.4 %wave.1 = (f32[8,128,128]{2,1,0:T(8,128)}, bf16[12,128,128]{2,1,0:T(8,128)(2,1)}, f32[12,8,128]{2,1,0:T(8,128)}) custom-call(f32[8,128,128]{2,1,0:T(8,128)} %c_ref.1, f32[8,128,128]{2,1,0:T(8,128)} %wave_prev.1, f32[8,128,128]{2,1,0:T(8,128)} %wave_now.1, f32[8,128,128]{2,1,0:T(8,128)} %adj_late.1, f32[8,128,128]{2,1,0:T(8,128)} %adj_last.1, f32[12]{0:T(128)} %wavelet.1, ...), custom_call_target="tpu_custom_call" | custom-call | tf_op jit(solution)/shard_map/wave/pallas_call | solution.py:322
  147.2 0.0 copy-start.11
  147.2 0.7 copy-done.11
  147.9 0.0 copy-start.10
  147.9 0.7 copy-done.10
  148.6 0.3 convolution_bitcast_fusion.1
  148.9 0.0 copy-start.12
  148.9 0.2 reshape.46.w3
  149.1 0.5 copy-done.12
  149.6 0.1 copy.29
  149.7 0.0 copy-start.8
  149.7 0.7 copy-done.8
  150.4 0.3 convolution_bitcast_fusion
  150.7 0.1 copy.31
  150.8 0.3 reshape.43
  151.2 0.0 copy-start.9
  151.2 0.0 copy-start.14
  151.2 0.1 copy.34.w1
  151.3 0.5 copy-done.9
  151.9 0.0 copy-done.14
  151.9 0.0 copy-start.15
  151.9 0.0 copy-start.16
  151.9 0.1 multiply_bitcast_fusion
  152.0 0.0 copy-start
  152.0 0.0 copy-start.1
  152.0 0.4 reshape.44.w2
  152.4 0.2 copy-done.15
  152.5 0.2 broadcast_in_dim_tile.8.b1
  152.7 0.0 copy-done.16
  152.7 0.2 broadcast_in_dim_tile.9.b2
  153.5 0.0 copy-done
  153.5 0.0 copy-done.1
  153.6 0.0 copy-start.2
  153.6 23.4 %prior.1.model = bf16[8,128,128]{2,1,0:T(8,128)(2,1)S(1)} custom-call(bf16[12,128,128]{2,1,0:T(8,128)(2,1)S(1)} %copy-done.1, f32[8,128,128]{2,1,0:T(8,128)S(1)} %copy-done, bf16[320,144]{1,0:T(8,128)(2,1)S(1)} %copy.34.w1, bf16[256,256]{1,0:T(8,128)(2,1)S(1)} %reshape.44.w2, bf16[72,320]{1,0:T(8,128)(2,1)S(1)} %reshape.46.w3, ...), custom_call_target="tpu_custom_call" | custom-call | tf_op jit(solution)/shard_map/prior/pallas_call | solution.py:467
  177.0 0.0 copy-done.2
  177.0 0.1 copy.37.owner_sub
  177.1 0.0 copy-start.3
  177.1 0.7 copy-done.3
  177.8 0.0 copy-start.5
  177.8 17.3 %route.1 = bf16[16,16,1024]{2,1,0:T(8,128)(2,1)S(1)} custom-call(bf16[8,128,128]{2,1,0:T(8,128)(2,1)S(1)} %prior.1.model, s32[128,1]{1,0:T(8,128)S(1)} %copy.37.owner_sub, s32[1,128]{1,0:T(1,128)S(1)} %bitcast.41, s32[1,128]{1,0:T(1,128)S(1)} %bitcast.42), custom_call_target="tpu_custom_call" | custom-call | tf_op jit(solution)/shard_map/route/pallas_call | solution.py:545
  195.1 0.0 copy-done.5
  195.1 0.6 copy.41
  195.7 0.8 copy.53
  (9 shorter events, 0.1 us)
Async XLA Ops:
  0.6 0.7 copy-start.13
  1.3 1.0 copy-start.7
  1.3 1.0 copy-start.6
  2.4 1.0 copy-start.4
  147.2 0.7 copy-start.11
  147.9 0.7 copy-start.10
  148.9 0.7 copy-start.12
  149.7 0.7 copy-start.8
  151.2 0.7 copy-start.9
  151.2 0.7 copy-start.14
  151.9 0.7 copy-start.15
  151.9 0.8 copy-start.16
  152.0 1.6 copy-start
  152.0 1.6 copy-start.1
  153.6 23.4 %copy-start.2 = (s32[128,1]{0,1:T(1,128)S(1)}, s32[128,1]{0,1:T(1,128)}, u32[]{:S(2)}) copy-start(s32[128,1]{0,1:T(1,128)} %param.30) | copy-start | bytes 1540
  177.1 0.7 copy-start.3
  177.8 17.3 %copy-start.5 = (f32[12,8,128]{2,1,0:T(8,128)S(1)}, f32[12,8,128]{2,1,0:T(8,128)}, u32[]{:S(2)}) copy-start(f32[12,8,128]{2,1,0:T(8,128)} %get-tuple-element.5) | copy-start | bytes 147460
where the time goes:
time: 197 us
  Pallas kernels  183 us (93%)
  local copies, waits for them, and re-layouts  10.5 us (5%)
  between operations  2.2 us (1%)
    pallas_call x1, Pallas kernels, wave(): pl.pallas_call(functools.partial(wave_kernel, n), out_shape=(jax.ShapeDty...  142 us
    pallas_call x1, Pallas kernels, prior(): pl.pallas_call(prior_kernel, out_shape=jax.ShapeDtypeStruct((cx, ny, nz),...  23.4 us
    pallas_call x1, Pallas kernels, route(): pl.pallas_call(functools.partial(route_kernel, n, cap), out_shape=jax.Sha...  17.3 us
    unnamed x40, local copies, waits for them, and re-layouts  6.3 us

commit v1 on v0

--- a/solution.py
+++ b/solution.py
@@ -8,7 +8,6 @@
 from jax.sharding import PartitionSpec as P
 
 MESH = pl.DeviceIdType.MESH
-PAD = 8
 
 
 def wave_kernel(
@@ -40,6 +39,9 @@
     zhot_t,
     parts,
     inj_parts,
+    band_z,
+    band_y,
+    lap_yz,
     rec_send,
     rec_recv,
     resid8,
@@ -63,8 +65,9 @@
     barrier = pltpu.get_barrier_semaphore()
 
     for buf in (fwd, adj):
-        for k in range(3):
-            buf[k] = jnp.zeros(buf.shape[1:], jnp.float32)
+        for k in range(1, 4):
+            buf[k % 3, 0:2] = jnp.zeros((2, ny, nz), jnp.float32)
+            buf[k % 3, cx + 2 : cx + 4] = jnp.zeros((2, ny, nz), jnp.float32)
     wide_ref[0:2] = jnp.zeros((2, ny, nz), jnp.bfloat16)
     wide_ref[cx + 2 : cx + 4] = jnp.zeros((2, ny, nz), jnp.bfloat16)
     def greet(d, carry):
@@ -75,12 +78,11 @@
 
     lax.fori_loop(1, n, greet, 0)
 
-    inner = pl.ds(PAD, ny)
     for i in range(cx):
-        fwd[0, i + 2, inner] = wave_prev[i]
-        fwd[1, i + 2, inner] = wave_now[i]
-        adj[0, i + 2, inner] = adj_late[i]
-        adj[1, i + 2, inner] = adj_last[i]
+        fwd[0, i + 2] = wave_prev[i]
+        fwd[1, i + 2] = wave_now[i]
+        adj[0, i + 2] = adj_late[i]
+        adj[1, i + 2] = adj_last[i]
     pl.semaphore_wait(barrier, n - 1)
 
     def halo(buf, k, send, recv, up):
@@ -88,8 +90,8 @@
         to = 0 if up else cx + 2
         side = 1 if up else 0
         return pltpu.make_async_remote_copy(
-            src_ref=buf.at[k, pl.ds(lo, 2), inner],
-            dst_ref=buf.at[k, pl.ds(to, 2), inner],
+            src_ref=buf.at[k, pl.ds(lo, 2)],
+            dst_ref=buf.at[k, pl.ds(to, 2)],
             send_sem=send.at[side],
             recv_sem=recv.at[k, side],
             device_id=(shot, me + 1 if up else me - 1),
@@ -146,21 +148,42 @@
         lax.broadcasted_iota(jnp.int32, (nz, nrec), 0) == z_lane[...], 1.0, 0.0
     )
 
+    across = lax.broadcasted_iota(jnp.int32, (2 * nz, nz), 0) % nz
+    gap = jnp.abs(across - lax.broadcasted_iota(jnp.int32, (2 * nz, nz), 1))
+    band_z[...] = (
+        jnp.where(gap == 1, 16.0, 0.0) - jnp.where(gap == 2, 1.0, 0.0)
+    ).astype(jnp.bfloat16)
+    across = lax.broadcasted_iota(jnp.int32, (ny, 2 * ny), 1) % ny
+    gap = jnp.abs(across - lax.broadcasted_iota(jnp.int32, (ny, 2 * ny), 0))
+    band_y[...] = (
+        jnp.where(gap == 1, 16.0, 0.0) - jnp.where(gap == 2, 1.0, 0.0)
+    ).astype(jnp.bfloat16)
+
     chunk = 32
-    lane = lax.broadcasted_iota(jnp.int32, (chunk, nz), 1)
-
-    def laplace12(buf, k, i, y):
-        def at(plane, dy):
-            return buf[k, plane, pl.ds(PAD + y + dy, chunk), :]
-
-        mid = at(i + 2, 0)
-        near = (at(i + 3, 0) + at(i + 1, 0)) + (at(i + 2, 1) + at(i + 2, -1))
-        far = (at(i + 4, 0) + at(i, 0)) + (at(i + 2, 2) + at(i + 2, -2))
-        near += jnp.where(lane >= 1, pltpu.roll(mid, 1, 1), 0.0)
-        near += jnp.where(lane < nz - 1, pltpu.roll(mid, nz - 1, 1), 0.0)
-        far += jnp.where(lane >= 2, pltpu.roll(mid, 2, 1), 0.0)
-        far += jnp.where(lane < nz - 2, pltpu.roll(mid, nz - 2, 1), 0.0)
-        return mid, 16.0 * near - far - 90.0 * mid
+
+    def split(i, y, value):
+        high = value.astype(jnp.bfloat16)
+        at = pl.ds(i * ny + y, chunk)
+        parts[at, 0:nz] = high
+        parts[at, nz : 2 * nz] = (value - high.astype(jnp.float32)).astype(jnp.bfloat16)
+
+    def along_yz(buf, k):
+        for i in range(cx):
+            at = pl.ds(i * ny, ny)
+            z_part = jnp.dot(parts[at, :], band_z[...], preferred_element_type=jnp.float32)
+            both = jnp.concatenate([parts[at, 0:nz], parts[at, nz : 2 * nz]], axis=0)
+            y_part = jnp.dot(band_y[...], both, preferred_element_type=jnp.float32)
+            lap_yz[i] = z_part + y_part - 90.0 * buf[k, i + 2]
+
+    def lap_at(buf, k, i, y):
+        at = pl.ds(y, chunk)
+        near = buf[k, i + 3, at] + buf[k, i + 1, at]
+        far = buf[k, i + 4, at] + buf[k, i, at]
+        return buf[k, i + 2, at], lap_yz[i, at] + (16.0 * near - far)
+
+    for i in range(cx):
+        for y in range(0, ny, chunk):
+            split(i, y, wave_now[i, pl.ds(y, chunk)])
 
     order = [0, 1, cx - 2, cx - 1] + list(range(2, cx - 2))
 
@@ -181,20 +204,17 @@
     def forward(t, carry):
         prev, cur, nxt = lax.rem(t, 3), lax.rem(t + 1, 3), lax.rem(t + 2, 3)
         impulse = wavelet[t]
+        along_yz(fwd, cur)
         wait_side(fwd, cur, f_send, f_recv)
         for done, i in enumerate(order):
             for y in range(0, ny, chunk):
-                mid, lap = laplace12(fwd, cur, i, y)
+                mid, lap = lap_at(fwd, cur, i, y)
                 at = pl.ds(y, chunk)
                 change = c12[i, at] * lap + impulse * src[i, at]
                 changes[t, i, at] = change
-                newest = 2.0 * mid - fwd[prev, i + 2, pl.ds(PAD + y, chunk)] + change
-                fwd[nxt, i + 2, pl.ds(PAD + y, chunk)] = newest
-                high = newest.astype(jnp.bfloat16)
-                parts[pl.ds(i * ny + y, chunk), 0:nz] = high
-                parts[pl.ds(i * ny + y, chunk), nz : 2 * nz] = (
-                    newest - high.astype(jnp.float32)
-                ).astype(jnp.bfloat16)
+                newest = 2.0 * mid - fwd[prev, i + 2, at] + change
+                fwd[nxt, i + 2, at] = newest
+                split(i, y, newest)
             if done == 1:
 
                 @pl.when(t < steps - 1)
@@ -225,10 +245,13 @@
 
     for i in range(cx):
         grad_ref[i] = jnp.zeros((ny, nz), jnp.float32)
+        for y in range(0, ny, chunk):
+            split(i, y, adj_last[i, pl.ds(y, chunk)])
 
     def backward(s, carry):
         t = steps - 1 - s
         prev, cur, nxt = lax.rem(s, 3), lax.rem(s + 1, 3), lax.rem(s + 2, 3)
+        along_yz(adj, cur)
         arrived = rec_recv.at[t]
         pltpu.make_async_copy(arrived, arrived, r_recv.at[t]).wait()
         pltpu.make_async_copy(arrived, arrived, r_send.at[t]).wait()
@@ -249,14 +272,15 @@
         wait_side(adj, cur, a_send, a_recv)
         for done, i in enumerate(order):
             for y in range(0, ny, chunk):
-                mid, lap = laplace12(adj, cur, i, y)
+                mid, lap = lap_at(adj, cur, i, y)
                 at = pl.ds(y, chunk)
                 newest = (
                     2.0 * mid
-                    - adj[prev, i + 2, pl.ds(PAD + y, chunk)]
+                    - adj[prev, i + 2, at]
                     + (c12[i, at] * lap + inj[pl.ds(i * ny + y, chunk), :])
                 )
-                adj[nxt, i + 2, pl.ds(PAD + y, chunk)] = newest
+                adj[nxt, i + 2, at] = newest
+                split(i, y, newest)
                 grad_ref[i, at] = grad_ref[i, at] + newest * changes[t, i, at]
             if done == 1:
 
@@ -329,8 +353,8 @@
         in_specs=[vmem] * 5 + [smem] * 2 + [vmem] * 5,
         out_specs=(vmem, vmem, vmem),
         scratch_shapes=[
-            pltpu.VMEM((3, cx + 4, ny + 2 * PAD, nz), f32),
-            pltpu.VMEM((3, cx + 4, ny + 2 * PAD, nz), f32),
+            pltpu.VMEM((3, cx + 4, ny, nz), f32),
+            pltpu.VMEM((3, cx + 4, ny, nz), f32),
             pltpu.VMEM((steps, cx, ny, nz), f32),
             pltpu.VMEM((cx, ny, nz), f32),
             pltpu.VMEM((cx, ny, nz), f32),
@@ -341,6 +365,9 @@
             pltpu.VMEM((nz, nrec), f32),
             pltpu.VMEM((rows, 2 * nz), bf16),
             pltpu.VMEM((2 * nz, nrec), bf16),
+            pltpu.VMEM((2 * nz, nz), bf16),
+            pltpu.VMEM((ny, 2 * ny), bf16),
+            pltpu.VMEM((cx, ny, nz), f32),
             pltpu.VMEM((steps, groups, 128), f32),
             pltpu.VMEM((steps, n - 1, groups, 128), f32),
             pltpu.VMEM((groups, 128), f32),

time: 197 us -> 172 us (0.87)
  Pallas kernels: 183 us -> 158 us
    pallas_call x1, Pallas kernels: 142 us -> 119 us  [wave(): pl.pallas_call(functools.partial(wave_kernel, n), out_shape=(jax.ShapeDty...]
where the time goes in v1:
time: 172 us
  Pallas kernels  158 us (92%)
  local copies, waits for them, and re-layouts  10.5 us (6%)
  between operations  2.2 us (1%)
    pallas_call x1, Pallas kernels, wave(): pl.pallas_call(functools.partial(wave_kernel, n), out_shape=(jax.ShapeDty...  119 us
    pallas_call x1, Pallas kernels, prior(): pl.pallas_call(prior_kernel, out_shape=jax.ShapeDtypeStruct((cx, ny, nz),...  23.4 us
    pallas_call x1, Pallas kernels, route(): pl.pallas_call(functools.partial(route_kernel, n, cap), out_shape=jax.Sha...  16.3 us
    unnamed x40, local copies, waits for them, and re-layouts  6.3 us

profile of v1, /device:TPU:13, one launch (start us, length us, event | category | flops | bytes accessed | tf_op | source)
XLA Modules:
  0.0 171.9 jit_solution(11498376284219375414)
XLA Ops:
  0.6 0.0 copy-start.13
  0.6 0.7 copy-done.13
  1.3 0.0 copy-start.7
  1.3 0.0 copy-start.6
  1.4 1.0 copy.27.row_sub
  2.4 0.0 copy-done.7
  2.4 0.0 copy-done.6
  2.4 0.0 copy-start.4
  2.4 1.0 copy.28.z_sub
  3.4 0.0 copy-done.4
  3.4 0.6 slice.observed
  4.7 118.8 %wave.1 = (f32[8,128,128]{2,1,0:T(8,128)}, bf16[12,128,128]{2,1,0:T(8,128)(2,1)}, f32[12,8,128]{2,1,0:T(8,128)}) custom-call(f32[8,128,128]{2,1,0:T(8,128)} %c_ref.1, f32[8,128,128]{2,1,0:T(8,128)} %wave_prev.1, f32[8,128,128]{2,1,0:T(8,128)} %wave_now.1, f32[8,128,128]{2,1,0:T(8,128)} %adj_late.1, f32[8,128,128]{2,1,0:T(8,128)} %adj_last.1, f32[12]{0:T(128)} %wavelet.1, ...), custom_call_target="tpu_custom_call" | custom-call | tf_op jit(solution)/shard_map/wave/pallas_call | solution.py:346
  123.5 0.0 copy-start.11
  123.5 0.7 copy-done.11
  124.2 0.0 copy-start.10
  124.2 0.7 copy-done.10
  124.9 0.3 convolution_bitcast_fusion.1
  125.2 0.0 copy-start.12
  125.2 0.2 reshape.46.w3
  125.4 0.5 copy-done.12
  125.9 0.1 copy.29
  126.0 0.0 copy-start.8
  126.0 0.7 copy-done.8
  126.7 0.3 convolution_bitcast_fusion
  127.0 0.1 copy.31
  127.2 0.3 reshape.43
  127.5 0.0 copy-start.9
  127.5 0.0 copy-start.14
  127.5 0.1 copy.34.w1
  127.7 0.5 copy-done.9
  128.2 0.0 copy-done.14
  128.2 0.0 copy-start.15
  128.2 0.0 copy-start.16
  128.2 0.1 multiply_bitcast_fusion
  128.3 0.0 copy-start
  128.3 0.0 copy-start.1
  128.3 0.4 reshape.44.w2
  128.7 0.2 copy-done.15
  128.9 0.2 broadcast_in_dim_tile.8.b1
  129.0 0.0 copy-done.16
  129.1 0.2 broadcast_in_dim_tile.9.b2
  129.9 0.0 copy-done
  129.9 0.0 copy-done.1
  129.9 0.0 copy-start.2
  129.9 23.4 %prior.1.model = bf16[8,128,128]{2,1,0:T(8,128)(2,1)S(1)} custom-call(bf16[12,128,128]{2,1,0:T(8,128)(2,1)S(1)} %copy-done.1, f32[8,128,128]{2,1,0:T(8,128)S(1)} %copy-done, bf16[320,144]{1,0:T(8,128)(2,1)S(1)} %copy.34.w1, bf16[256,256]{1,0:T(8,128)(2,1)S(1)} %reshape.44.w2, bf16[72,320]{1,0:T(8,128)(2,1)S(1)} %reshape.46.w3, ...), custom_call_target="tpu_custom_call" | custom-call | tf_op jit(solution)/shard_map/prior/pallas_call | solution.py:494
  153.3 0.0 copy-done.2
  153.4 0.1 copy.37.owner_sub
  153.5 0.0 copy-start.3
  153.5 0.7 copy-done.3
  154.1 0.0 copy-start.5
  154.1 16.3 %route.1 = bf16[16,16,1024]{2,1,0:T(8,128)(2,1)S(1)} custom-call(bf16[8,128,128]{2,1,0:T(8,128)(2,1)S(1)} %prior.1.model, s32[128,1]{1,0:T(8,128)S(1)} %copy.37.owner_sub, s32[1,128]{1,0:T(1,128)S(1)} %bitcast.41, s32[1,128]{1,0:T(1,128)S(1)} %bitcast.42), custom_call_target="tpu_custom_call" | custom-call | tf_op jit(solution)/shard_map/route/pallas_call | solution.py:572
  170.4 0.0 copy-done.5
  170.4 0.6 copy.41
  171.1 0.8 copy.53
  (9 shorter events, 0.1 us)
Async XLA Ops:
  0.6 0.7 copy-start.13
  1.3 1.0 copy-start.7
  1.3 1.0 copy-start.6
  2.4 1.0 copy-start.4
  123.5 0.7 copy-start.11
  124.2 0.7 copy-start.10
  125.2 0.7 copy-start.12
  126.0 0.7 copy-start.8
  127.5 0.7 copy-start.9
  127.5 0.7 copy-start.14
  128.2 0.7 copy-start.15
  128.2 0.8 copy-start.16
  128.3 1.6 copy-start
  128.3 1.6 copy-start.1
  129.9 23.4 %copy-start.2 = (s32[128,1]{0,1:T(1,128)S(1)}, s32[128,1]{0,1:T(1,128)}, u32[]{:S(2)}) copy-start(s32[128,1]{0,1:T(1,128)} %param.30) | copy-start | bytes 1540
  153.5 0.7 copy-start.3
  154.1 16.3 %copy-start.5 = (f32[12,8,128]{2,1,0:T(8,128)S(1)}, f32[12,8,128]{2,1,0:T(8,128)}, u32[]{:S(2)}) copy-start(f32[12,8,128]{2,1,0:T(8,128)} %get-tuple-element.5) | copy-start | bytes 147460

commit v2 on v1

--- a/solution.py
+++ b/solution.py
@@ -85,39 +85,35 @@
         adj[1, i + 2] = adj_last[i]
     pl.semaphore_wait(barrier, n - 1)
 
-    def halo(buf, k, send, recv, up):
+    def halo(buf, k, send, recv, up, plane):
         lo = cx if up else 2
         to = 0 if up else cx + 2
         side = 1 if up else 0
         return pltpu.make_async_remote_copy(
-            src_ref=buf.at[k, pl.ds(lo, 2)],
-            dst_ref=buf.at[k, pl.ds(to, 2)],
-            send_sem=send.at[side],
-            recv_sem=recv.at[k, side],
+            src_ref=buf.at[k, lo + plane],
+            dst_ref=buf.at[k, to + plane],
+            send_sem=send.at[side, plane],
+            recv_sem=recv.at[k, side, plane],
             device_id=(shot, me + 1 if up else me - 1),
             device_id_type=MESH,
         )
 
-    def start_side(buf, k, send, recv, up):
+    def start_side(buf, k, send, recv, up, plane):
         @pl.when((me < n - 1) if up else (me > 0))
         def _():
-            halo(buf, k, send, recv, up).start()
-
-    def wait_side(buf, k, send, recv):
-        @pl.when(me < n - 1)
+            halo(buf, k, send, recv, up, plane).start()
+
+    def wait_side(buf, k, send, recv, low):
+        @pl.when((me > 0) if low else (me < n - 1))
         def _():
-            halo(buf, k, send, recv, True).wait_send()
-            halo(buf, k, send, recv, False).wait_recv()
-
-        @pl.when(me > 0)
-        def _():
-            halo(buf, k, send, recv, False).wait_send()
-            halo(buf, k, send, recv, True).wait_recv()
-
-    for up in (False, True):
-        start_side(fwd, 1, f_send, f_recv, up)
-    for up in (False, True):
-        start_side(adj, 1, a_send, a_recv, up)
+            for plane in range(2):
+                halo(buf, k, send, recv, not low, plane).wait_send()
+                halo(buf, k, send, recv, low, plane).wait_recv()
+
+    for buf, send, recv in ((fwd, f_send, f_recv), (adj, a_send, a_recv)):
+        for up in (False, True):
+            for plane in range(2):
+                start_side(buf, 1, send, recv, up, plane)
 
     for i in range(cx):
         c12[i] = c_ref[i] * (1.0 / 12.0)
@@ -205,8 +201,9 @@
         prev, cur, nxt = lax.rem(t, 3), lax.rem(t + 1, 3), lax.rem(t + 2, 3)
         impulse = wavelet[t]
         along_yz(fwd, cur)
-        wait_side(fwd, cur, f_send, f_recv)
         for done, i in enumerate(order):
+            if done == 0 or done == 2:
+                wait_side(fwd, cur, f_send, f_recv, done == 0)
             for y in range(0, ny, chunk):
                 mid, lap = lap_at(fwd, cur, i, y)
                 at = pl.ds(y, chunk)
@@ -215,17 +212,11 @@
                 newest = 2.0 * mid - fwd[prev, i + 2, at] + change
                 fwd[nxt, i + 2, at] = newest
                 split(i, y, newest)
-            if done == 1:
+            if done < 4:
 
                 @pl.when(t < steps - 1)
                 def _():
-                    start_side(fwd, nxt, f_send, f_recv, False)
-
-            if done == 3:
-
-                @pl.when(t < steps - 1)
-                def _():
-                    start_side(fwd, nxt, f_send, f_recv, True)
+                    start_side(fwd, nxt, f_send, f_recv, done >= 2, done % 2)
 
         picked = jnp.dot(hot_t[...], parts[...], preferred_element_type=jnp.float32)
         zsel = zhot[...]
@@ -269,8 +260,9 @@
             hot[...], inj_parts[...], (((1,), (1,)), ((), ())), preferred_element_type=jnp.float32
         )
         inj[...] = spread[:, 0:nz] + spread[:, nz : 2 * nz]
-        wait_side(adj, cur, a_send, a_recv)
         for done, i in enumerate(order):
+            if done == 0 or done == 2:
+                wait_side(adj, cur, a_send, a_recv, done == 0)
             for y in range(0, ny, chunk):
                 mid, lap = lap_at(adj, cur, i, y)
                 at = pl.ds(y, chunk)
@@ -282,17 +274,11 @@
                 adj[nxt, i + 2, at] = newest
                 split(i, y, newest)
                 grad_ref[i, at] = grad_ref[i, at] + newest * changes[t, i, at]
-            if done == 1:
+            if done < 4:
 
                 @pl.when(s < steps - 1)
                 def _():
-                    start_side(adj, nxt, a_send, a_recv, False)
-
-            if done == 3:
-
-                @pl.when(s < steps - 1)
-                def _():
-                    start_side(adj, nxt, a_send, a_recv, True)
+                    start_side(adj, nxt, a_send, a_recv, done >= 2, done % 2)
 
         return carry
 
@@ -371,10 +357,10 @@
             pltpu.VMEM((steps, groups, 128), f32),
             pltpu.VMEM((steps, n - 1, groups, 128), f32),
             pltpu.VMEM((groups, 128), f32),
-            pltpu.SemaphoreType.DMA((2,)),
-            pltpu.SemaphoreType.DMA((3, 2)),
-            pltpu.SemaphoreType.DMA((2,)),
-            pltpu.SemaphoreType.DMA((3, 2)),
+            pltpu.SemaphoreType.DMA((2, 2)),
+            pltpu.SemaphoreType.DMA((3, 2, 2)),
+            pltpu.SemaphoreType.DMA((2, 2)),
+            pltpu.SemaphoreType.DMA((3, 2, 2)),
             pltpu.SemaphoreType.DMA((steps,)),
             pltpu.SemaphoreType.DMA((steps,)),
             pltpu.SemaphoreType.DMA((2,)),

time: 172 us -> 174 us (1.012)
  Pallas kernels: 158 us -> 160 us
where the time goes in v2:
time: 174 us
  Pallas kernels  160 us (92%)
  local copies, waits for them, and re-layouts  10.5 us (6%)
  between operations  2.2 us (1%)
    pallas_call x1, Pallas kernels, wave(): pl.pallas_call(functools.partial(wave_kernel, n), out_shape=(jax.ShapeDty...  119 us
    pallas_call x1, Pallas kernels, prior(): pl.pallas_call(prior_kernel, out_shape=jax.ShapeDtypeStruct((cx, ny, nz),...  23.4 us
    pallas_call x1, Pallas kernels, route(): pl.pallas_call(functools.partial(route_kernel, n, cap), out_shape=jax.Sha...  17.6 us
    unnamed x40, local copies, waits for them, and re-layouts  6.3 us

profile of v2, /device:TPU:13, one launch (start us, length us, event | category | flops | bytes accessed | tf_op | source)
XLA Modules:
  0.0 173.8 jit_solution(7649000764290429289)
XLA Ops:
  0.6 0.0 copy-start.13
  0.6 0.7 copy-done.13
  1.3 0.0 copy-start.7
  1.3 0.0 copy-start.6
  1.4 1.0 copy.27.row_sub
  2.4 0.0 copy-done.7
  2.4 0.0 copy-done.6
  2.4 0.0 copy-start.4
  2.4 1.0 copy.28.z_sub
  3.4 0.0 copy-done.4
  3.4 0.6 slice.observed
  4.7 119.4 %wave.1 = (f32[8,128,128]{2,1,0:T(8,128)}, bf16[12,128,128]{2,1,0:T(8,128)(2,1)}, f32[12,8,128]{2,1,0:T(8,128)}) custom-call(f32[8,128,128]{2,1,0:T(8,128)} %c_ref.1, f32[8,128,128]{2,1,0:T(8,128)} %wave_prev.1, f32[8,128,128]{2,1,0:T(8,128)} %wave_now.1, f32[8,128,128]{2,1,0:T(8,128)} %adj_late.1, f32[8,128,128]{2,1,0:T(8,128)} %adj_last.1, f32[12]{0:T(128)} %wavelet.1, ...), custom_call_target="tpu_custom_call" | custom-call | tf_op jit(solution)/shard_map/wave/pallas_call | solution.py:332
  124.1 0.0 copy-start.11
  124.2 0.7 copy-done.11
  124.8 0.0 copy-start.10
  124.8 0.7 copy-done.10
  125.5 0.3 convolution_bitcast_fusion.1
  125.8 0.0 copy-start.12
  125.9 0.2 reshape.46.w3
  126.0 0.5 copy-done.12
  126.5 0.1 copy.29
  126.6 0.0 copy-start.8
  126.7 0.7 copy-done.8
  127.3 0.3 convolution_bitcast_fusion
  127.7 0.1 copy.31
  127.8 0.3 reshape.43
  128.1 0.0 copy-start.9
  128.1 0.0 copy-start.14
  128.2 0.1 copy.34.w1
  128.3 0.5 copy-done.9
  128.8 0.0 copy-done.14
  128.8 0.0 copy-start.15
  128.8 0.0 copy-start.16
  128.8 0.1 multiply_bitcast_fusion
  128.9 0.0 copy-start
  129.0 0.0 copy-start.1
  129.0 0.4 reshape.44.w2
  129.3 0.2 copy-done.15
  129.5 0.2 broadcast_in_dim_tile.8.b1
  129.7 0.0 copy-done.16
  129.7 0.2 broadcast_in_dim_tile.9.b2
  130.5 0.0 copy-done
  130.5 0.0 copy-done.1
  130.5 0.0 copy-start.2
  130.5 23.4 %prior.1.model = bf16[8,128,128]{2,1,0:T(8,128)(2,1)S(1)} custom-call(bf16[12,128,128]{2,1,0:T(8,128)(2,1)S(1)} %copy-done.1, f32[8,128,128]{2,1,0:T(8,128)S(1)} %copy-done, bf16[320,144]{1,0:T(8,128)(2,1)S(1)} %copy.34.w1, bf16[256,256]{1,0:T(8,128)(2,1)S(1)} %reshape.44.w2, bf16[72,320]{1,0:T(8,128)(2,1)S(1)} %reshape.46.w3, ...), custom_call_target="tpu_custom_call" | custom-call | tf_op jit(solution)/shard_map/prior/pallas_call | solution.py:480
  154.0 0.0 copy-done.2
  154.0 0.1 copy.37.owner_sub
  154.1 0.0 copy-start.3
  154.1 0.7 copy-done.3
  154.7 0.0 copy-start.5
  154.7 17.6 %route.1 = bf16[16,16,1024]{2,1,0:T(8,128)(2,1)S(1)} custom-call(bf16[8,128,128]{2,1,0:T(8,128)(2,1)S(1)} %prior.1.model, s32[128,1]{1,0:T(8,128)S(1)} %copy.37.owner_sub, s32[1,128]{1,0:T(1,128)S(1)} %bitcast.41, s32[1,128]{1,0:T(1,128)S(1)} %bitcast.42), custom_call_target="tpu_custom_call" | custom-call | tf_op jit(solution)/shard_map/route/pallas_call | solution.py:558
  172.4 0.0 copy-done.5
  172.4 0.6 copy.41
  173.0 0.8 copy.53
  (9 shorter events, 0.1 us)
Async XLA Ops:
  0.6 0.7 copy-start.13
  1.3 1.0 copy-start.7
  1.3 1.0 copy-start.6
  2.4 1.0 copy-start.4
  124.1 0.7 copy-start.11
  124.8 0.7 copy-start.10
  125.8 0.7 copy-start.12
  126.6 0.7 copy-start.8
  128.1 0.7 copy-start.9
  128.1 0.7 copy-start.14
  128.8 0.7 copy-start.15
  128.8 0.8 copy-start.16
  128.9 1.6 copy-start
  129.0 1.6 copy-start.1
  130.5 23.4 %copy-start.2 = (s32[128,1]{0,1:T(1,128)S(1)}, s32[128,1]{0,1:T(1,128)}, u32[]{:S(2)}) copy-start(s32[128,1]{0,1:T(1,128)} %param.30) | copy-start | bytes 1540
  154.1 0.7 copy-start.3
  154.7 17.6 %copy-start.5 = (f32[12,8,128]{2,1,0:T(8,128)S(1)}, f32[12,8,128]{2,1,0:T(8,128)}, u32[]{:S(2)}) copy-start(f32[12,8,128]{2,1,0:T(8,128)} %get-tuple-element.5) | copy-start | bytes 147460
